TPU v7x, 32 devices: a whole 2x2x4 slice. The times are simulated.
32 devices in a mesh: frame: 8 (over y, x, core), row: 4 (over z).
Axes of the slice: x: 2, y: 2, z: 4, core: 2. Of those that a mesh axis runs over, the one named last changes fastest.
Arguments:
- query_raw: bfloat16 [8192, 1120], P(('frame', 'row')), may hold values from -6 to 6
- key_raw: bfloat16 [8192, 1120], P(('frame', 'row')), may hold values from -6 to 6
- values: bfloat16 [8192, 1120], P(('frame', 'row')), may hold values from -6 to 6
- norm_gain: float32 [1120], replicated, may hold values from 0.1 to 1.9
- grad_out: bfloat16 [8192, 1120], P(('frame', 'row')), may hold values from -6 to 6
Outputs:
- grad_query: bfloat16 [8192, 1120], P(('frame', 'row'))
- grad_key: bfloat16 [8192, 1120], P(('frame', 'row'))
- grad_value: bfloat16 [8192, 1120], P(('frame', 'row'))
All inputs are finite; a program needn't handle non-finite values.
Results may differ from a plain program's by a relative error of at most 0.018.
Values may be sent and summed in bfloat16 or wider, within the bound.
A program may use at most 64 MiB of HBM per device.

v0:
```python
import jax
import jax.numpy as jnp
from jax import lax
from jax.sharding import PartitionSpec as P

HEAD_DIM = 112


def feature(raw_values):
    return jnp.where(raw_values > 0, raw_values + 1.0, jnp.exp(jnp.minimum(raw_values, 0.0)))


def slope_of(raw_values):
    return jnp.where(raw_values > 0, 1.0, jnp.exp(jnp.minimum(raw_values, 0.0)))


def padded_flat(state, row_size):
    flat = state.reshape(state.shape[0] * state.shape[1], state.shape[2])
    rows_all = flat.shape[0]
    rows_padded = -(-rows_all // row_size) * row_size
    return jnp.pad(flat, ((0, rows_padded - rows_all), (0, 0)))


def body(query_raw, key_raw, values, norm_gain, grad_out):
    tok_rows = query_raw.shape[0]
    width_all = query_raw.shape[1]
    head_size = HEAD_DIM
    head_count = width_all // head_size
    split_shape = (tok_rows, head_count, head_size)
    state_shape = (head_count, head_size, head_size)
    rows_all = head_count * head_size
    row_size = lax.axis_size("row")
    frame_own = lax.axis_index("frame")
    query_float = query_raw.astype(jnp.float32).reshape(split_shape)
    key_float = key_raw.astype(jnp.float32).reshape(split_shape)
    query_feat = feature(query_float).astype(jnp.bfloat16)
    key_feat = feature(key_float).astype(jnp.bfloat16)
    value_heads = values.reshape(split_shape)
    local_state = jnp.einsum(
        "thi,thj->hij", key_feat, value_heads, preferred_element_type=jnp.float32
    )
    state_share = lax.psum_scatter(
        padded_flat(local_state, row_size), "row", scatter_dimension=0, tiled=True
    )
    piece = lax.all_gather(state_share[None], "frame", axis=0, tiled=True)
    blocks = jnp.arange(piece.shape[0], dtype=jnp.int32)
    keep = (blocks <= frame_own).astype(jnp.float32)
    state_share = jnp.sum(keep[:, None, None] * piece, axis=0)
    prefix_whole = lax.all_gather(state_share.astype(jnp.bfloat16), "row", axis=0, tiled=True)
    prefix_low = prefix_whole[:rows_all].reshape(state_shape)
    attention = jnp.einsum(
        "thi,hij->thj", query_feat, prefix_low, preferred_element_type=jnp.float32
    )
    mean_square = jnp.mean(attention * attention, axis=-1, keepdims=True)
    inv_rms = lax.rsqrt(mean_square + 1e-06)
    weighted = grad_out.reshape(split_shape).astype(jnp.float32) * norm_gain.reshape(
        head_count, head_size
    )
    inner = jnp.mean(weighted * attention, axis=-1, keepdims=True)
    grad_attention = (inv_rms * weighted - attention * inv_rms * inv_rms * inv_rms * inner).astype(
        jnp.bfloat16
    )
    grad_qfeat = jnp.einsum(
        "thj,hij->thi", grad_attention, prefix_low, preferred_element_type=jnp.float32
    )
    grad_q = (grad_qfeat * slope_of(query_float)).astype(jnp.bfloat16).reshape(tok_rows, width_all)
    local_adjoint = jnp.einsum(
        "thi,thj->hij", query_feat, grad_attention, preferred_element_type=jnp.float32
    )
    adjoint_share = lax.psum_scatter(
        padded_flat(local_adjoint, row_size).astype(jnp.bfloat16),
        "row",
        scatter_dimension=0,
        tiled=True,
    ).astype(jnp.float32)
    piece = lax.all_gather(
        adjoint_share[None].astype(jnp.bfloat16), "frame", axis=0, tiled=True
    ).astype(jnp.float32)
    blocks = jnp.arange(piece.shape[0], dtype=jnp.int32)
    keep = (blocks >= frame_own).astype(jnp.float32)
    adjoint_share = jnp.zeros_like(adjoint_share) + jnp.sum(keep[:, None, None] * piece, axis=0)
    adjoint_whole = lax.all_gather(adjoint_share.astype(jnp.bfloat16), "row", axis=0, tiled=True)
    adjoint_low = adjoint_whole[:rows_all].reshape(state_shape)
    grad_v = jnp.einsum("thi,hij->thj", key_feat, adjoint_low, preferred_element_type=jnp.float32)
    grad_v = grad_v.astype(jnp.bfloat16).reshape(tok_rows, width_all)
    grad_kfeat = jnp.einsum(
        "thj,hij->thi", value_heads, adjoint_low, preferred_element_type=jnp.float32
    )
    grad_k = (grad_kfeat * slope_of(key_float)).astype(jnp.bfloat16).reshape(tok_rows, width_all)
    return (grad_q, grad_k, grad_v)


def solution(mesh):
    return jax.shard_map(
        body,
        mesh=mesh,
        in_specs=(
            P(("frame", "row"), None),
            P(("frame", "row"), None),
            P(("frame", "row"), None),
            P(),
            P(("frame", "row"), None),
        ),
        out_specs=(P(("frame", "row"), None), P(("frame", "row"), None), P(("frame", "row"), None)),
        check_vma=False,
    )
```

profile of v0, /device:TPU:0, one launch (start us, length us, event | category | flops | bytes accessed | tf_op | source)
XLA Modules:
  0.0 116.2 jit_solution(14152594329269913379)
XLA Ops:
  7.2 0.0 copy-start
  7.2 0.0 reduce-scatter.7.cloned.1.call-start
  7.2 1.4 %fusion.7 = (f32[256,1120]{0,1:T(8,128)S(1)}, bf16[256,1120]{0,1:T(8,128)(2,1)S(1)}) fusion(bf16[256,1120]{0,1:T(8,128)(2,1)} %param.6), kind=kLoop, calls=%fused_computation.18 | loop fusion | flops 2007040 | bytes 2293760 | tf_op jit(solution)/shard_map/jit(_where)/select_n | solution.py:14
  8.7 0.0 copy-done
  8.7 0.0 copy-start.5
  8.7 0.0 copy-start.4
  8.7 1.1 fusion.18
  9.8 0.0 reduce-scatter.7.cloned.1.call-update
  9.8 0.0 reduce-scatter.9.cloned.1.call-start
  9.9 0.0 copy-done.5
  9.9 0.1 mul.76
  10.0 0.0 copy-done.4
  10.0 1.3 %fusion.9 = (bf16[256,1120]{0,1:T(8,128)(2,1)S(1)}, f32[256,1120]{0,1:T(8,128)}) fusion(bf16[256,1120]{0,1:T(8,128)(2,1)S(1)} %copy-done.4), kind=kLoop, calls=%fused_computation.20 | loop fusion | flops 2007040 | bytes 2293760 | tf_op jit(solution)/shard_map/convert_element_type | solution.py:36
  11.3 0.0 copy-start.2
  11.3 24.3 %reduce-scatter.7.cloned.1.call-done = f32[280,112]{1,0:T(8,128)} async-done(((f32[1120,112]{1,0:T(8,128)}), f32[280,112]{1,0:T(8,128)}) %reduce-scatter.7.cloned.1.call-update) | async-done | bytes 125456
  35.6 11.5 %all-gather = f32[2240,112]{1,0:T(8,128)S(1)} all-gather(f32[280,112]{1,0:T(8,128)} %reduce-scatter.7.cloned.1.call-done), channel_id=2, replica_groups=mesh['frame'=8,'row'=4] {'frame'}, dimensions={0}, use_global_device_ids=true | all-gather | bytes 1128960 | tf_op jit(solution)/shard_map/all_gather | solution.py:45
  47.1 0.2 multiply_reduce_fusion.1
  47.3 14.6 %all_gather.13 = bf16[1120,112]{1,0:T(8,128)(2,1)S(1)} all-gather(bf16[280,112]{1,0:T(8,128)(2,1)S(1)} %multiply_reduce_fusion.1), channel_id=1, replica_groups=mesh['frame'=8,'row'=4] {'row'}, dimensions={0}, use_global_device_ids=true | all-gather | bytes 313600 | tf_op jit(solution)/shard_map/all_gather | solution.py:49
  61.9 0.0 copy-done.2
  61.9 0.5 multiply_reduce_fusion
  62.4 0.2 copy-done.1
  62.7 0.4 copy-done.3
  63.1 0.4 fusion.16
  63.5 1.0 convolution_convert_fusion.1
  64.5 0.0 reduce-scatter.9.cloned.1.call-update
  64.5 2.5 %fusion.2 = bf16[256,10,112]{0,2,1:T(8,128)(2,1)} fusion(f32[256,10,112]{0,2,1:T(8,128)} %bitcast.53, bf16[10,112,112]{2,1,0:T(8,128)(2,1)} %bitcast.56, bf16[256,10,112]{0,2,1:T(8,128)(2,1)S(1)} %fusion.16), kind=kOutput, calls=%fused_computation.12 | convolution fusion | flops 64798720 | bytes 2544640 | tf_op jit(solution)/shard_map/thj,hij->thi/dot_general | solution.py:63
  67.0 15.4 %reduce-scatter.9.cloned.1.call-done = bf16[280,112]{1,0:T(8,128)(2,1)} async-done(((bf16[1120,112]{1,0:T(8,128)(2,1)}), bf16[280,112]{1,0:T(8,128)(2,1)}) %reduce-scatter.9.cloned.1.call-update) | async-done | bytes 62736
  82.4 9.9 %all-gather.1 = bf16[2240,112]{1,0:T(8,128)(2,1)S(1)} all-gather(bf16[280,112]{1,0:T(8,128)(2,1)} %reduce-scatter.9.cloned.1.call-done), channel_id=3, replica_groups=mesh['frame'=8,'row'=4] {'frame'}, dimensions={0}, use_global_device_ids=true | all-gather | bytes 564480 | tf_op jit(solution)/shard_map/all_gather | solution.py:76
  92.3 0.2 fusion.12
  92.5 14.6 %all_gather.15 = bf16[1120,112]{1,0:T(8,128)(2,1)S(1)} all-gather(bf16[280,112]{1,0:T(8,128)(2,1)S(1)} %fusion.12), channel_id=1, replica_groups=mesh['frame'=8,'row'=4] {'row'}, dimensions={0}, use_global_device_ids=true | all-gather | bytes 313600 | tf_op jit(solution)/shard_map/all_gather | solution.py:82
  107.1 1.2 %convolution_convert_fusion = bf16[10,112,256]{2,1,0:T(8,128)(2,1)} fusion(bf16[10,112,112]{2,1,0:T(8,128)(2,1)S(1)} %bitcast.57, bf16[256,10,112]{0,2,1:T(8,128)(2,1)S(1)} %bitcast.51), kind=kOutput, calls=%fused_computation.11 | convolution fusion | flops 64512000 | bytes 1397760 | tf_op jit(solution)/shard_map/thi,hij->thj/dot_general | solution.py:84
  108.3 1.1 fusion.3
  (5 shorter events, 0.0 us)
Async XLA Ops:
  7.2 1.5 %copy-start = (bf16[256,1120]{0,1:T(8,128)(2,1)S(1)}, bf16[256,1120]{0,1:T(8,128)(2,1)}, u32[]{:S(2)}) copy-start(bf16[256,1120]{0,1:T(8,128)(2,1)} %param.7) | copy-start | bytes 1720324
  7.2 28.4 %reduce-scatter.7.cloned.1.call-start = ((), (), s32[]{:S(2)}) async-start(), calls=%async_computation.2 | async-start | bytes 716800
  8.7 1.2 %copy-start.5 = (f32[1120]{0:T(1024)S(1)}, f32[1120]{0:T(1024)}, u32[]{:S(2)}) copy-start(f32[1120]{0:T(1024)} %param.8) | copy-start | bytes 13444
  8.7 1.3 %copy-start.4 = (bf16[256,1120]{0,1:T(8,128)(2,1)S(1)}, bf16[256,1120]{0,1:T(8,128)(2,1)}, u32[]{:S(2)}) copy-start(bf16[256,1120]{0,1:T(8,128)(2,1)} %param.5) | copy-start | bytes 1720324
  9.8 72.5 %reduce-scatter.9.cloned.1.call-start = ((), (), s32[]{:S(2)}) async-start(), calls=%async_computation.3 | async-start | bytes 358400
  11.3 50.6 %copy-start.2 = (bf16[256,1120]{0,1:T(8,128)(2,1)S(1)}, bf16[256,1120]{0,1:T(8,128)(2,1)}, u32[]{:S(2)}) copy-start(bf16[256,1120]{0,1:T(8,128)(2,1)} %param.9) | copy-start | bytes 1720324
  61.9 0.7 copy-start.1
  61.9 1.2 %copy-start.3 = (bf16[256,1120]{0,1:T(8,128)(2,1)S(1)}, bf16[256,1120]{0,1:T(8,128)(2,1)}, u32[]{:S(2)}) copy-start(bf16[256,1120]{0,1:T(8,128)(2,1)} %param.9) | copy-start | bytes 1720324
Sparse Core Ops, SparseCore 0:
  10.9 24.6 reduce-scatter.6
  64.7 17.6 reduce-scatter.8
where the time goes:
time: 117 us; the launch traced here: 116 us
  blocking collectives  50.7 us (43%)
  waiting for transfers between devices  39.7 us (34%)
  between operations  14.1 us (12%)
  matrix products  7.38 us (6%)
  other arithmetic  3.55 us (3%)
    unnamed x4, waiting for transfers between devices  39.7 us
    all_gather x1, blocking collectives, body(): lax.all_gather(state_share.astype(jnp.bfloat16), 'row', axis=0, tiled=True)  14.6 us
    all_gather x1, blocking collectives, body(): lax.all_gather(adjoint_share.astype(jnp.bfloat16), 'row', axis=0, tiled=T...  14.6 us
    all_gather x1, blocking collectives, body(): piece = lax.all_gather(state_share[None], 'frame', axis=0, tiled=True)  11.5 us
    all_gather x1, blocking collectives, body(): lax.all_gather(adjoint_share[None].astype(jnp.bfloat16), 'frame', axis=0,...  9.93 us
    dot_general x1, matrix products, body(): jnp.einsum('thj,hij->thi', grad_attention, prefix_low, preferred_element_...  2.47 us
  transfers between devices with their start and end apart: 2, of which 2 were waited for; matrix products, arithmetic and copies ran while one was open for 3% of the time, Pallas kernels for 0%

commit v1 on v0

v1 whole, which is shorter than its diff:
```python
import functools

import jax
import jax.numpy as jnp
from jax import lax
from jax.experimental import pallas as pl
from jax.experimental.pallas import tpu as pltpu
from jax.sharding import PartitionSpec as P

HEAD_DIM = 112
LANES = 128
MESH = pl.DeviceIdType.MESH
TN = (((0,), (0,)), ((), ()))
NT = (((1,), (1,)), ((), ()))
NN = (((1,), (0,)), ((), ()))


def dot(a, b, dims):
    return lax.dot_general(a, b, dims, preferred_element_type=jnp.float32)


def kernel(groups, piece, rows_n, frames_n, q_hbm, k_hbm, v_hbm, gain_ref, g_hbm,
           gq_hbm, gk_hbm, gv_hbm,
           q_raw, k_raw, v_raw, g_raw, gq_out, gk_out, gv_out,
           q_feat, k_feat, v_head, q_slope, k_slope, weighted, grad_att,
           send_buf, rs_buf, share, fr_send, fr_buf, ag_send, whole,
           in_sem, out_sem, rs_ssem, rs_rsem, fr_ssem, fr_rsem, ag_ssem, ag_rsem):
    D = HEAD_DIM
    owners = 2 * rows_n
    chips = frames_n // 2
    frame, row = lax.axis_index("frame"), lax.axis_index("row")
    chip, core = frame // 2, frame % 2
    me = row * 2 + core

    def column_id(step):
        dest = lax.rem(me + step, owners)
        return (chip * 2 + dest % 2, dest // 2)

    def chip_id(step):
        return (lax.rem(chip + step, chips) * 2 + core, row)

    loads = [
        pltpu.make_async_copy(src, dst, in_sem.at[i])
        for i, (src, dst) in enumerate(
            [(k_hbm, k_raw), (v_hbm, v_raw), (q_hbm, q_raw), (g_hbm, g_raw)])
    ]
    for c in loads:
        c.start()

    barrier = pltpu.get_barrier_semaphore()
    for j in range(1, owners):
        pl.semaphore_signal(barrier, inc=1, device_id=column_id(j), device_id_type=MESH)
    for j in range(1, chips):
        pl.semaphore_signal(barrier, inc=1, device_id=chip_id(j), device_id_type=MESH)

    def cols(h):
        return slice(h * D, (h + 1) * D)

    def phi(raw):
        low = jnp.exp(jnp.minimum(raw, 0.0))
        return jnp.where(raw > 0, raw + 1.0, low), jnp.where(raw > 0, 1.0, low)

    def rs_copy(p, g, j):
        dest = lax.rem(me + j, owners)
        return pltpu.make_async_remote_copy(
            src_ref=send_buf.at[p, g, pl.ds(pl.multiple_of(dest * piece, 16), piece)],
            dst_ref=rs_buf.at[p, g, j],
            send_sem=rs_ssem.at[p, g, j], recv_sem=rs_rsem.at[p, g, j],
            device_id=column_id(j), device_id_type=MESH)

    def fr_copy(p, g, j):
        return pltpu.make_async_remote_copy(
            src_ref=fr_send.at[p, g], dst_ref=fr_buf.at[p, g, j],
            send_sem=fr_ssem.at[p, g, j], recv_sem=fr_rsem.at[p, g, j],
            device_id=chip_id(j), device_id_type=MESH)

    def ag_copy(p, g, j):
        return pltpu.make_async_remote_copy(
            src_ref=ag_send.at[p, g, j % 2],
            dst_ref=whole.at[p, g, pl.ds(pl.multiple_of(me * piece, 16), piece)],
            send_sem=ag_ssem.at[p, g, j], recv_sem=ag_rsem.at[p, g, j],
            device_id=column_id(j), device_id_type=MESH)

    def ag_wait(p, g, j):
        src = lax.rem(me - j + owners, owners)
        pltpu.make_async_remote_copy(
            src_ref=ag_send.at[p, g, j % 2],
            dst_ref=whole.at[p, g, pl.ds(pl.multiple_of(src * piece, 16), piece)],
            send_sem=ag_ssem.at[p, g, j], recv_sem=ag_rsem.at[p, g, j],
            device_id=column_id(j), device_id_type=MESH).wait_recv()

    def start_rs(p, g):
        for j in range(1, owners):
            rs_copy(p, g, j).start()

    def reduce_rows(p, g):
        own = pl.ds(pl.multiple_of(me * piece, 16), piece)
        mine = send_buf[p, g, own, :].astype(jnp.float32)
        other = None
        for j in range(1, owners):
            rs_copy(p, g, j).wait_recv()
        for j in range(1, owners):
            block = rs_buf[p, g, j].astype(jnp.float32)
            if j % 2 == 0:
                mine = mine + block
            else:
                other = block if other is None else other + block
        share[p, g, 0] = mine
        share[p, g, 1] = other
        fr_send[p, g] = (mine + other).astype(jnp.bfloat16)
        for j in range(1, chips):
            fr_copy(p, g, j).start()

    def scan_frames(p, g):
        for j in range(1, chips):
            fr_copy(p, g, j).wait_recv()
        base = jnp.zeros((piece, LANES), jnp.float32)
        for j in range(1, chips):
            keep = (j <= chip) if p == 0 else (j > chip)
            base = base + jnp.where(keep, fr_buf[p, g, j].astype(jnp.float32), 0.0)
        mine, other = share[p, g, 0], share[p, g, 1]
        own_last = (core == 1) if p == 0 else (core == 0)
        ag_send[p, g, 0] = (base + mine + jnp.where(own_last, other, 0.0)).astype(jnp.bfloat16)
        ag_send[p, g, 1] = (base + other + jnp.where(own_last, 0.0, mine)).astype(jnp.bfloat16)
        for j in range(1, owners):
            ag_copy(p, g, j).start()
        own = pl.ds(pl.multiple_of(me * piece, 16), piece)
        whole[p, g, own, :] = ag_send[p, g, 0]

    def wait_whole(p, g):
        for j in range(1, owners):
            ag_wait(p, g, j)

    span = range(len(groups))

    def head_state(p, g, i):
        return whole[p, g, i * D:(i + 1) * D, :D]

    loads[0].wait()
    loads[1].wait()
    for g in span:
        for i, h in enumerate(groups[g]):
            feat, slope = phi(k_raw[:, cols(h)].astype(jnp.float32))
            feat = feat.astype(jnp.bfloat16)
            val = v_raw[:, cols(h)]
            k_feat[h] = feat
            k_slope[h] = slope
            v_head[h] = val
            send_buf[0, g, i * D:(i + 1) * D, :D] = dot(feat, val, TN).astype(jnp.bfloat16)
        if g == 0:
            pl.semaphore_wait(barrier, owners - 1 + chips - 1)
        start_rs(0, g)

    loads[2].wait()
    loads[3].wait()
    for g in span:
        for h in groups[g]:
            feat, slope = phi(q_raw[:, cols(h)].astype(jnp.float32))
            q_feat[h] = feat.astype(jnp.bfloat16)
            q_slope[h] = slope
            weighted[h] = g_raw[:, cols(h)].astype(jnp.float32) * gain_ref[:, cols(h)]

    for g in span:
        reduce_rows(0, g)
    for g in span:
        scan_frames(0, g)

    for g in span:
        wait_whole(0, g)
        for i, h in enumerate(groups[g]):
            att = dot(q_feat[h], head_state(0, g, i), NN)
            w = weighted[h]
            inv = lax.rsqrt(jnp.mean(att * att, axis=-1, keepdims=True) + 1e-6)
            inner = jnp.mean(w * att, axis=-1, keepdims=True)
            ga = (inv * w - att * (inv * inv * inv * inner)).astype(jnp.bfloat16)
            grad_att[h] = ga
            send_buf[1, g, i * D:(i + 1) * D, :D] = dot(q_feat[h], ga, TN).astype(jnp.bfloat16)
        start_rs(1, g)

    for g in span:
        for i, h in enumerate(groups[g]):
            gq = dot(grad_att[h], head_state(0, g, i), NT) * q_slope[h]
            gq_out[:, cols(h)] = gq.astype(jnp.bfloat16)
    stores = [
        pltpu.make_async_copy(src, dst, out_sem.at[i])
        for i, (src, dst) in enumerate([(gq_out, gq_hbm), (gk_out, gk_hbm), (gv_out, gv_hbm)])
    ]
    stores[0].start()

    for g in span:
        reduce_rows(1, g)
    for g in span:
        scan_frames(1, g)
    for g in span:
        wait_whole(1, g)
        for i, h in enumerate(groups[g]):
            adj = head_state(1, g, i)
            gv_out[:, cols(h)] = dot(k_feat[h], adj, NN).astype(jnp.bfloat16)
            gk_out[:, cols(h)] = (dot(v_head[h], adj, NT) * k_slope[h]).astype(jnp.bfloat16)
    stores[1].start()
    stores[2].start()

    for p in range(2):
        for g in span:
            for j in range(1, owners):
                rs_copy(p, g, j).wait_send()
                ag_copy(p, g, j).wait_send()
            for j in range(1, chips):
                fr_copy(p, g, j).wait_send()
    for c in stores:
        c.wait()


GROUPS = 2


def body(rows_n, frames_n, query_raw, key_raw, values, norm_gain, grad_out):
    tok, width = query_raw.shape
    heads = width // HEAD_DIM
    owners, chips = 2 * rows_n, frames_n // 2
    size = -(-heads // GROUPS)
    groups = [list(range(s, min(s + size, heads))) for s in range(0, heads, size)]
    n = len(groups)
    unit = 16 * owners
    piece = -(-size * HEAD_DIM // unit) * 16
    bf, f32 = jnp.bfloat16, jnp.float32
    raw = pltpu.VMEM((tok, width), bf)
    per_head = lambda t: pltpu.VMEM((heads, tok, HEAD_DIM), t)
    dma = pltpu.SemaphoreType.DMA
    out = jax.ShapeDtypeStruct((tok, width), bf)
    flops = 12 * tok * heads * HEAD_DIM * HEAD_DIM
    hbm = pl.BlockSpec(memory_space=pl.ANY)
    return pl.pallas_call(
        functools.partial(kernel, groups, piece, rows_n, frames_n),
        out_shape=(out, out, out),
        in_specs=[hbm, hbm, hbm, pl.BlockSpec(memory_space=pltpu.VMEM), hbm],
        out_specs=(hbm, hbm, hbm),
        scratch_shapes=[
            raw, raw, raw, raw, raw, raw, raw,
            per_head(bf), per_head(bf), per_head(bf), per_head(f32), per_head(f32),
            per_head(f32), per_head(bf),
            pltpu.VMEM((2, n, owners * piece, LANES), bf),
            pltpu.VMEM((2, n, owners, piece, LANES), bf),
            pltpu.VMEM((2, n, 2, piece, LANES), f32),
            pltpu.VMEM((2, n, piece, LANES), bf),
            pltpu.VMEM((2, n, chips, piece, LANES), bf),
            pltpu.VMEM((2, n, 2, piece, LANES), bf),
            pltpu.VMEM((2, n, owners * piece, LANES), bf),
            dma((4,)), dma((3,)),
            dma((2, n, owners)), dma((2, n, owners)),
            dma((2, n, chips)), dma((2, n, chips)),
            dma((2, n, owners)), dma((2, n, owners)),
        ],
        cost_estimate=pl.CostEstimate(
            flops=flops, bytes_accessed=14 * tok * width, transcendentals=2 * tok * width),
        compiler_params=pltpu.CompilerParams(
            collective_id=0, has_side_effects=True, vmem_limit_bytes=48 * 1024 * 1024),
    )(query_raw, key_raw, values, norm_gain.reshape(1, width), grad_out)


def solution(mesh):
    split = P(("frame", "row"), None)
    return jax.shard_map(
        functools.partial(body, mesh.shape["row"], mesh.shape["frame"]),
        mesh=mesh,
        in_specs=(split, split, split, P(), split),
        out_specs=(split, split, split),
        check_vma=False,
    )
```

time: 117 us -> 54.2 us (0.46)
  blocking collectives: 50.7 us -> 0 us
  Pallas kernels: 0 us -> 43.7 us
  waiting for transfers between devices: 39.7 us -> 0 us
  between operations: 14.1 us -> 0.67 us
  local copies, waits for them, and re-layouts: 0.76 us -> 9.55 us
  matrix products: 7.38 us -> 0 us
  other arithmetic: 3.55 us -> 0 us
    all_gather x4 -> x0, blocking collectives: 50.7 us -> none  [the longest x1 14.6 us: body(): lax.all_gather(state_share.astype(jnp.bfloat16), 'row', axis=0, tiled=True)]
    pallas_call x0 -> x1, Pallas kernels: none -> 43.7 us  [body(): pl.pallas_call(functools.partial(kernel, groups, piece, rows_n, frames_n)...]
    unnamed x4 -> x0, waiting for transfers between devices: 39.7 us -> none
    dot_general x6 -> x0, matrix products: 7.38 us -> none  [the longest x1 2.47 us: body(): jnp.einsum('thj,hij->thi', grad_attention, prefix_low, preferred_element_...]
    pallas_call x0 -> x3, local copies, waits for them, and re-layouts: none -> 4.2 us  [body(): pl.pallas_call(functools.partial(kernel, groups, piece, rows_n, frames_n)...]
    unnamed x12, local copies, waits for them, and re-layouts: 0.68 us -> 4.64 us
    convert_element_type x4 -> x0, other arithmetic: 1.71 us -> none  [the longest x1 1.33 us: body(): query_feat = feature(query_float).astype(jnp.bfloat16)]
    select_n x1 -> x0, other arithmetic: 1.43 us -> none  [slope_of(): return jnp.where(raw_values > 0, 1.0, jnp.exp(jnp.minimum(raw_values, 0.0)))]
  transfers between devices with their start and end apart: 2 -> 0, of which waited for: 2 -> 0; matrix products, arithmetic and copies ran while one was open for 3% -> 0% of each run, Pallas kernels for 0% -> 0%
where the time goes in v1:
time: 54.2 us; the launch traced here: 53.9 us
  Pallas kernels  43.7 us (81%)
  local copies, waits for them, and re-layouts  9.55 us (18%)
  between operations  0.67 us (1%)
    pallas_call x1, Pallas kernels, body(): pl.pallas_call(functools.partial(kernel, groups, piece, rows_n, frames_n)...  43.7 us
    unnamed x12, local copies, waits for them, and re-layouts  4.64 us
    pallas_call x3, local copies, waits for them, and re-layouts, body(): pl.pallas_call(functools.partial(kernel, groups, piece, rows_n, frames_n)...  4.2 us

profile of v1, /device:TPU:0, one launch (start us, length us, event | category | flops | bytes accessed | tf_op | source)
XLA Modules:
  0.0 53.9 jit_solution(16502167378869585444)
XLA Ops:
  0.6 0.7 %reshape.9.gain_ref = f32[1,1120]{1,0:T(1,128)S(1)} reshape(f32[1120]{0:T(1024)} %param.8) | data formatting | bytes 8960 | tf_op jit(solution)/shard_map/reshape | solution.py:258
  1.3 0.0 copy-start.1
  1.3 1.4 %copy.8.q_hbm = bf16[256,1120]{1,0:T(8,128)(2,1)S(1)} copy(bf16[256,1120]{0,1:T(8,128)(2,1)} %param.5) | data formatting | bytes 1146880 | tf_op args[0]
  2.7 0.0 copy-done.1
  2.8 0.0 copy-start.2
  2.8 0.3 copy.9.k_hbm
  3.1 0.8 %copy-done.2 = bf16[256,1120]{0,1:T(8,128)(2,1)S(1)} copy-done((bf16[256,1120]{0,1:T(8,128)(2,1)S(1)}, bf16[256,1120]{0,1:T(8,128)(2,1)}, u32[]{:S(2)}) %copy-start.2) | copy-done | bytes 573464
  3.8 0.0 copy-start.3
  3.8 0.3 copy.10.v_hbm
  4.1 0.8 %copy-done.3 = bf16[256,1120]{0,1:T(8,128)(2,1)S(1)} copy-done((bf16[256,1120]{0,1:T(8,128)(2,1)S(1)}, bf16[256,1120]{0,1:T(8,128)(2,1)}, u32[]{:S(2)}) %copy-start.3) | copy-done | bytes 573464
  4.9 0.3 copy.11.g_hbm
  5.2 43.7 %shard_map.76 = (bf16[256,1120]{1,0:T(8,128)(2,1)S(1)}, bf16[256,1120]{1,0:T(8,128)(2,1)S(1)}, bf16[256,1120]{1,0:T(8,128)(2,1)S(1)}) custom-call(bf16[256,1120]{1,0:T(8,128)(2,1)S(1)} %copy.8.q_hbm, bf16[256,1120]{1,0:T(8,128)(2,1)S(1)} %copy.9.k_hbm, bf16[256,1120]{1,0:T(8,128)(2,1)S(1)} %copy.10.v_hbm, f32[1,1120]{1,0:T(1,128)S(1)} %reshape.9.gain_ref, ...), custom_call_target="tpu_custom_call" | custom-call | flops 385351680 | bytes 4014080 | tf_op jit(solution)/shard_map/pallas_call | solution.py:233
  48.9 0.0 copy-start
  48.9 0.8 %copy-done = bf16[256,1120]{1,0:T(8,128)(2,1)} copy-done((bf16[256,1120]{1,0:T(8,128)(2,1)}, bf16[256,1120]{1,0:T(8,128)(2,1)S(1)}, u32[]{:S(2)}) %copy-start) | copy-done | bytes 573464
  49.7 2.1 %copy.12 = bf16[256,1120]{0,1:T(8,128)(2,1)} copy(bf16[256,1120]{1,0:T(8,128)(2,1)} %copy-done) | data formatting | bytes 1146880 | tf_op jit(solution)/shard_map/pallas_call | solution.py:233
  51.8 1.1 %copy.13 = bf16[256,1120]{0,1:T(8,128)(2,1)} copy(bf16[256,1120]{1,0:T(8,128)(2,1)S(1)} %get-tuple-element.4) | data formatting | bytes 1146880 | tf_op jit(solution)/shard_map/pallas_call | solution.py:233
  52.9 1.1 %copy.14 = bf16[256,1120]{0,1:T(8,128)(2,1)} copy(bf16[256,1120]{1,0:T(8,128)(2,1)S(1)} %get-tuple-element.5) | data formatting | bytes 1146880 | tf_op jit(solution)/shard_map/pallas_call | solution.py:233
Async XLA Ops:
  1.3 1.4 %copy-start.1 = (bf16[256,1120]{0,1:T(8,128)(2,1)S(1)}, bf16[256,1120]{0,1:T(8,128)(2,1)}, u32[]{:S(2)}) copy-start(bf16[256,1120]{0,1:T(8,128)(2,1)} %param.6) | copy-start | bytes 1720324
  2.8 1.1 %copy-start.2 = (bf16[256,1120]{0,1:T(8,128)(2,1)S(1)}, bf16[256,1120]{0,1:T(8,128)(2,1)}, u32[]{:S(2)}) copy-start(bf16[256,1120]{0,1:T(8,128)(2,1)} %param.7) | copy-start | bytes 1720324
  3.8 1.1 %copy-start.3 = (bf16[256,1120]{0,1:T(8,128)(2,1)S(1)}, bf16[256,1120]{0,1:T(8,128)(2,1)}, u32[]{:S(2)}) copy-start(bf16[256,1120]{0,1:T(8,128)(2,1)} %param.9) | copy-start | bytes 1720324
  48.9 0.8 %copy-start = (bf16[256,1120]{1,0:T(8,128)(2,1)}, bf16[256,1120]{1,0:T(8,128)(2,1)S(1)}, u32[]{:S(2)}) copy-start(bf16[256,1120]{1,0:T(8,128)(2,1)S(1)} %get-tuple-element.3) | copy-start | bytes 1720324

commit v2 on v1

v2 whole, which is shorter than its diff:
```python
import functools

import jax
import jax.numpy as jnp
from jax import lax
from jax.experimental import pallas as pl
from jax.experimental.pallas import tpu as pltpu
from jax.sharding import PartitionSpec as P

HEAD_DIM = 112
LANES = 128
MESH = pl.DeviceIdType.MESH
TN = (((0,), (0,)), ((), ()))
NT = (((1,), (1,)), ((), ()))
NN = (((1,), (0,)), ((), ()))


def dot(a, b, dims):
    return lax.dot_general(a, b, dims, preferred_element_type=jnp.float32)


def kernel(groups, pieces, rows_n, frames_n, q_hbm, k_hbm, v_hbm, gain_ref, g_hbm,
           gq_hbm, gk_hbm, gv_hbm,
           q_raw, k_raw, v_raw, g_raw, gq_out, gk_out, gv_out,
           q_feat, k_feat, gain, q_slope, k_slope, weighted, grad_att,
           send_buf, rs_buf, share, fr_send, fr_buf, ag_send, whole,
           in_sem, out_sem, rs_ssem, rs_rsem, fr_ssem, fr_rsem, ag_ssem, ag_rsem):
    D = HEAD_DIM
    owners = 2 * rows_n
    chips = frames_n // 2
    frame, row = lax.axis_index("frame"), lax.axis_index("row")
    chip, core = frame // 2, frame % 2
    me = row * 2 + core

    def column_id(step):
        dest = lax.rem(me + step, owners)
        return (chip * 2 + dest % 2, dest // 2)

    def chip_id(step):
        return (lax.rem(chip + step, chips) * 2 + core, row)

    loads = [
        pltpu.make_async_copy(src, dst, in_sem.at[i])
        for i, (src, dst) in enumerate(
            [(k_hbm, k_raw), (v_hbm, v_raw), (q_hbm, q_raw), (g_hbm, g_raw)])
    ]
    for c in loads:
        c.start()

    barrier = pltpu.get_barrier_semaphore()
    for j in range(1, owners):
        pl.semaphore_signal(barrier, inc=1, device_id=column_id(j), device_id_type=MESH)
    for j in range(1, chips):
        pl.semaphore_signal(barrier, inc=1, device_id=chip_id(j), device_id_type=MESH)

    def cols(h):
        return slice(h * D, (h + 1) * D)

    base_of = [sum(pieces[:g]) * owners for g in range(len(groups))]
    slot_of = [sum(pieces[:g]) for g in range(len(groups))]

    def rows_of(g, index):
        return pl.ds(pl.multiple_of(base_of[g] + index * pieces[g], 16), pieces[g])

    def slot(g):
        return pl.ds(slot_of[g], pieces[g])

    def phi(raw):
        low = jnp.exp(jnp.minimum(raw, 0.0))
        return jnp.where(raw > 0, raw + 1.0, low), jnp.where(raw > 0, 1.0, low)

    def rs_copy(p, g, j):
        dest = lax.rem(me + j, owners)
        return pltpu.make_async_remote_copy(
            src_ref=send_buf.at[p, rows_of(g, dest)],
            dst_ref=rs_buf.at[p, j, slot(g)],
            send_sem=rs_ssem.at[p, g, j], recv_sem=rs_rsem.at[p, g, j],
            device_id=column_id(j), device_id_type=MESH)

    def fr_copy(p, g, j):
        return pltpu.make_async_remote_copy(
            src_ref=fr_send.at[p, slot(g)], dst_ref=fr_buf.at[p, j, slot(g)],
            send_sem=fr_ssem.at[p, g, j], recv_sem=fr_rsem.at[p, g, j],
            device_id=chip_id(j), device_id_type=MESH)

    def ag_copy(p, g, j):
        return pltpu.make_async_remote_copy(
            src_ref=ag_send.at[p, j % 2, slot(g)],
            dst_ref=whole.at[p, rows_of(g, me)],
            send_sem=ag_ssem.at[p, g, j], recv_sem=ag_rsem.at[p, g, j],
            device_id=column_id(j), device_id_type=MESH)

    def ag_wait(p, g, j):
        src = lax.rem(me - j + owners, owners)
        pltpu.make_async_remote_copy(
            src_ref=ag_send.at[p, j % 2, slot(g)],
            dst_ref=whole.at[p, rows_of(g, src)],
            send_sem=ag_ssem.at[p, g, j], recv_sem=ag_rsem.at[p, g, j],
            device_id=column_id(j), device_id_type=MESH).wait_recv()

    def start_rs(p, g):
        for j in range(1, owners):
            rs_copy(p, g, j).start()

    def reduce_rows(p, g):
        mine = send_buf[p, rows_of(g, me), :].astype(jnp.float32)
        other = None
        for j in range(1, owners):
            rs_copy(p, g, j).wait_recv()
        for j in range(1, owners):
            block = rs_buf[p, j, slot(g), :].astype(jnp.float32)
            if j % 2 == 0:
                mine = mine + block
            else:
                other = block if other is None else other + block
        share[p, 0, slot(g), :] = mine
        share[p, 1, slot(g), :] = other
        fr_send[p, slot(g), :] = (mine + other).astype(jnp.bfloat16)
        for j in range(1, chips):
            fr_copy(p, g, j).start()

    def scan_frames(p, g):
        for j in range(1, chips):
            fr_copy(p, g, j).wait_recv()
        base = jnp.zeros((pieces[g], LANES), jnp.float32)
        for j in range(1, chips):
            keep = (j <= chip) if p == 0 else (j > chip)
            base = base + jnp.where(keep, fr_buf[p, j, slot(g), :].astype(jnp.float32), 0.0)
        mine, other = share[p, 0, slot(g), :], share[p, 1, slot(g), :]
        own_last = (core == 1) if p == 0 else (core == 0)
        ag_send[p, 0, slot(g), :] = (base + mine + jnp.where(own_last, other, 0.0)).astype(jnp.bfloat16)
        ag_send[p, 1, slot(g), :] = (base + other + jnp.where(own_last, 0.0, mine)).astype(jnp.bfloat16)
        for j in range(1, owners):
            ag_copy(p, g, j).start()
        whole[p, rows_of(g, me), :] = ag_send[p, 0, slot(g), :]

    def wait_whole(p, g):
        for j in range(1, owners):
            ag_wait(p, g, j)

    span = range(len(groups))

    def head_state(p, g, i):
        return whole[p, base_of[g] + i * D:base_of[g] + (i + 1) * D, :D]

    loads[0].wait()
    loads[1].wait()
    for g in span:
        for i, h in enumerate(groups[g]):
            feat, slope = phi(k_raw[cols(h), :].astype(jnp.float32))
            feat = feat.astype(jnp.bfloat16)
            val = v_raw[cols(h), :]
            k_feat[h] = feat
            k_slope[h] = slope
            send_buf[0, base_of[g] + i * D:base_of[g] + (i + 1) * D, :D] = dot(feat, val, NT).astype(jnp.bfloat16)
        if g == 0:
            pl.semaphore_wait(barrier, owners - 1 + chips - 1)
        start_rs(0, g)

    loads[2].wait()
    loads[3].wait()
    tok, width = q_raw.shape[1], q_raw.shape[0]
    gain[...] = jnp.broadcast_to(gain_ref[...].reshape(1, width), (tok, width)).T
    for g in span:
        for h in groups[g]:
            feat, slope = phi(q_raw[cols(h), :].astype(jnp.float32))
            q_feat[h] = feat.astype(jnp.bfloat16)
            q_slope[h] = slope
            weighted[h] = g_raw[cols(h), :].astype(jnp.float32) * gain[cols(h), :]

    for g in span:
        reduce_rows(0, g)
    for g in span:
        scan_frames(0, g)

    for g in span:
        wait_whole(0, g)
        for i, h in enumerate(groups[g]):
            att = dot(head_state(0, g, i), q_feat[h], TN)
            w = weighted[h]
            inv = lax.rsqrt(jnp.mean(att * att, axis=0, keepdims=True) + 1e-6)
            inner = jnp.mean(w * att, axis=0, keepdims=True)
            ga = (inv * w - att * (inv * inv * inv * inner)).astype(jnp.bfloat16)
            grad_att[h] = ga
            send_buf[1, base_of[g] + i * D:base_of[g] + (i + 1) * D, :D] = dot(q_feat[h], ga, NT).astype(jnp.bfloat16)
        start_rs(1, g)

    for g in span:
        for i, h in enumerate(groups[g]):
            gq = dot(head_state(0, g, i), grad_att[h], NN) * q_slope[h]
            gq_out[cols(h), :] = gq.astype(jnp.bfloat16)
    stores = [
        pltpu.make_async_copy(src, dst, out_sem.at[i])
        for i, (src, dst) in enumerate([(gq_out, gq_hbm), (gk_out, gk_hbm), (gv_out, gv_hbm)])
    ]
    stores[0].start()

    for g in span:
        reduce_rows(1, g)
    for g in span:
        scan_frames(1, g)
    for g in span:
        wait_whole(1, g)
        for i, h in enumerate(groups[g]):
            adj = head_state(1, g, i)
            gv_out[cols(h), :] = dot(adj, k_feat[h], TN).astype(jnp.bfloat16)
            gk_out[cols(h), :] = (dot(adj, v_raw[cols(h), :], NN) * k_slope[h]).astype(jnp.bfloat16)
    stores[1].start()
    stores[2].start()

    for p in range(2):
        for g in span:
            for j in range(1, owners):
                rs_copy(p, g, j).wait_send()
                ag_copy(p, g, j).wait_send()
            for j in range(1, chips):
                fr_copy(p, g, j).wait_send()
    for c in stores:
        c.wait()


def body(rows_n, frames_n, query_raw, key_raw, values, norm_gain, grad_out):
    tok, width = query_raw.shape
    heads = width // HEAD_DIM
    owners, chips = 2 * rows_n, frames_n // 2
    first = max(1, heads * 4 // 5)
    groups = [g for g in (list(range(first)), list(range(first, heads))) if g]
    n = len(groups)
    unit = 16 * owners
    pieces = [-(-len(g) * HEAD_DIM // unit) * 16 for g in groups]
    piece = sum(pieces)
    bf, f32 = jnp.bfloat16, jnp.float32
    raw = pltpu.VMEM((width, tok), bf)
    per_head = lambda t: pltpu.VMEM((heads, HEAD_DIM, tok), t)
    dma = pltpu.SemaphoreType.DMA
    out = jax.ShapeDtypeStruct((width, tok), bf)
    flops = 12 * tok * heads * HEAD_DIM * HEAD_DIM
    hbm = pl.BlockSpec(memory_space=pl.ANY)
    grads = pl.pallas_call(
        functools.partial(kernel, groups, pieces, rows_n, frames_n),
        out_shape=(out, out, out),
        in_specs=[hbm, hbm, hbm, pl.BlockSpec(memory_space=pltpu.VMEM), hbm],
        out_specs=(hbm, hbm, hbm),
        scratch_shapes=[
            raw, raw, raw, raw, raw, raw, raw,
            per_head(bf), per_head(bf), pltpu.VMEM((width, tok), f32),
            per_head(f32), per_head(f32), per_head(f32), per_head(bf),
            pltpu.VMEM((2, owners * piece, LANES), bf),
            pltpu.VMEM((2, owners, piece, LANES), bf),
            pltpu.VMEM((2, 2, piece, LANES), f32),
            pltpu.VMEM((2, piece, LANES), bf),
            pltpu.VMEM((2, chips, piece, LANES), bf),
            pltpu.VMEM((2, 2, piece, LANES), bf),
            pltpu.VMEM((2, owners * piece, LANES), bf),
            dma((4,)), dma((3,)),
            dma((2, n, owners)), dma((2, n, owners)),
            dma((2, n, chips)), dma((2, n, chips)),
            dma((2, n, owners)), dma((2, n, owners)),
        ],
        cost_estimate=pl.CostEstimate(
            flops=flops, bytes_accessed=14 * tok * width, transcendentals=2 * tok * width),
        compiler_params=pltpu.CompilerParams(
            collective_id=0, has_side_effects=True, vmem_limit_bytes=48 * 1024 * 1024),
    )(query_raw.T, key_raw.T, values.T, norm_gain, grad_out.T)
    return tuple(g.T for g in grads)


def solution(mesh):
    split = P(("frame", "row"), None)
    return jax.shard_map(
        functools.partial(body, mesh.shape["row"], mesh.shape["frame"]),
        mesh=mesh,
        in_specs=(split, split, split, P(), split),
        out_specs=(split, split, split),
        check_vma=False,
    )
```

time: 54.2 us -> 52.9 us (0.976)
  local copies, waits for them, and re-layouts: 9.55 us -> 7.35 us
  Pallas kernels: 43.7 us -> 44.6 us
    pallas_call x3 -> x0, local copies, waits for them, and re-layouts: 4.2 us -> none  [body(): pl.pallas_call(functools.partial(kernel, groups, piece, rows_n, frames_n)...]
    unnamed x12 -> x13, local copies, waits for them, and re-layouts: 4.64 us -> 7.35 us
    pallas_call x1, Pallas kernels: 43.7 us -> 44.6 us  [body(): pl.pallas_call(functools.partial(kernel, groups, pieces, rows_n, frames_n...]
    reshape x1 -> x0, local copies, waits for them, and re-layouts: 0.7 us -> none  [body(): norm_gain.reshape(1, width)]
where the time goes in v2:
time: 52.9 us; the launch traced here: 52.6 us
  Pallas kernels  44.6 us (84%)
  local copies, waits for them, and re-layouts  7.35 us (14%)
  between operations  0.65 us (1%)
    pallas_call x1, Pallas kernels, body(): pl.pallas_call(functools.partial(kernel, groups, pieces, rows_n, frames_n...  44.6 us
    unnamed x13, local copies, waits for them, and re-layouts  7.35 us

profile of v2, /device:TPU:0, one launch (start us, length us, event | category | flops | bytes accessed | tf_op | source)
XLA Modules:
  0.0 52.6 jit_solution(1850070607899332743)
XLA Ops:
  0.6 0.0 copy-start
  0.6 1.1 %copy-done = bf16[256,1120]{0,1:T(8,128)(2,1)S(1)} copy-done((bf16[256,1120]{0,1:T(8,128)(2,1)S(1)}, bf16[256,1120]{0,1:T(8,128)(2,1)}, u32[]{:S(2)}) %copy-start) | copy-done | bytes 573464
  1.7 0.0 copy-start.1
  1.7 1.1 %copy-done.1 = bf16[256,1120]{0,1:T(8,128)(2,1)S(1)} copy-done((bf16[256,1120]{0,1:T(8,128)(2,1)S(1)}, bf16[256,1120]{0,1:T(8,128)(2,1)}, u32[]{:S(2)}) %copy-start.1) | copy-done | bytes 573464
  2.8 0.0 copy-start.2
  2.8 1.1 %copy-done.2 = bf16[256,1120]{0,1:T(8,128)(2,1)S(1)} copy-done((bf16[256,1120]{0,1:T(8,128)(2,1)S(1)}, bf16[256,1120]{0,1:T(8,128)(2,1)}, u32[]{:S(2)}) %copy-start.2) | copy-done | bytes 573464
  3.8 0.0 copy-start.3
  3.8 1.1 %copy-done.3 = bf16[256,1120]{0,1:T(8,128)(2,1)S(1)} copy-done((bf16[256,1120]{0,1:T(8,128)(2,1)S(1)}, bf16[256,1120]{0,1:T(8,128)(2,1)}, u32[]{:S(2)}) %copy-start.3) | copy-done | bytes 573464
  4.9 0.0 copy-start.4
  4.9 0.7 %copy-done.4 = f32[1120]{0:T(1024)S(1)} copy-done((f32[1120]{0:T(1024)S(1)}, f32[1120]{0:T(1024)}, u32[]{:S(2)}) %copy-start.4) | copy-done | bytes 4504
  5.6 44.6 %shard_map.76 = (bf16[1120,256]{1,0:T(8,128)(2,1)S(1)}, bf16[1120,256]{1,0:T(8,128)(2,1)S(1)}, bf16[1120,256]{1,0:T(8,128)(2,1)S(1)}) custom-call(bf16[1120,256]{1,0:T(8,128)(2,1)S(1)} %bitcast.7, bf16[1120,256]{1,0:T(8,128)(2,1)S(1)} %bitcast.8, bf16[1120,256]{1,0:T(8,128)(2,1)S(1)} %bitcast.9, f32[1120]{0:T(1024)S(1)} %copy-done.4, ...), custom_call_target="tpu_custom_call" | custom-call | flops 385351680 | bytes 4014080 | tf_op jit(solution)/shard_map/pallas_call | solution.py:239
  50.2 0.8 %copy.11 = bf16[256,1120]{0,1:T(8,128)(2,1)} copy(bf16[256,1120]{0,1:T(8,128)(2,1)S(1)} %bitcast.13) | data formatting | bytes 1146880
  51.0 0.8 %copy.12 = bf16[256,1120]{0,1:T(8,128)(2,1)} copy(bf16[256,1120]{0,1:T(8,128)(2,1)S(1)} %bitcast.12) | data formatting | bytes 1146880
  51.8 0.8 %copy.13 = bf16[256,1120]{0,1:T(8,128)(2,1)} copy(bf16[256,1120]{0,1:T(8,128)(2,1)S(1)} %bitcast.11) | data formatting | bytes 1146880
Async XLA Ops:
  0.6 1.1 %copy-start = (bf16[256,1120]{0,1:T(8,128)(2,1)S(1)}, bf16[256,1120]{0,1:T(8,128)(2,1)}, u32[]{:S(2)}) copy-start(bf16[256,1120]{0,1:T(8,128)(2,1)} %param.5) | copy-start | bytes 1720324
  1.7 1.1 %copy-start.1 = (bf16[256,1120]{0,1:T(8,128)(2,1)S(1)}, bf16[256,1120]{0,1:T(8,128)(2,1)}, u32[]{:S(2)}) copy-start(bf16[256,1120]{0,1:T(8,128)(2,1)} %param.6) | copy-start | bytes 1720324
  2.8 1.1 %copy-start.2 = (bf16[256,1120]{0,1:T(8,128)(2,1)S(1)}, bf16[256,1120]{0,1:T(8,128)(2,1)}, u32[]{:S(2)}) copy-start(bf16[256,1120]{0,1:T(8,128)(2,1)} %param.7) | copy-start | bytes 1720324
  3.8 1.1 %copy-start.3 = (bf16[256,1120]{0,1:T(8,128)(2,1)S(1)}, bf16[256,1120]{0,1:T(8,128)(2,1)}, u32[]{:S(2)}) copy-start(bf16[256,1120]{0,1:T(8,128)(2,1)} %param.9) | copy-start | bytes 1720324
  4.9 0.7 %copy-start.4 = (f32[1120]{0:T(1024)S(1)}, f32[1120]{0:T(1024)}, u32[]{:S(2)}) copy-start(f32[1120]{0:T(1024)} %gain_ref.1) | copy-start | bytes 13444

commit v3 on v2

--- a/solution.py
+++ b/solution.py
@@ -9,6 +9,8 @@
 
 HEAD_DIM = 112
 LANES = 128
+OWNERS = 4
+GROUP = 4
 MESH = pl.DeviceIdType.MESH
 TN = (((0,), (0,)), ((), ()))
 NT = (((1,), (1,)), ((), ()))
@@ -23,18 +25,23 @@
            gq_hbm, gk_hbm, gv_hbm,
            q_raw, k_raw, v_raw, g_raw, gq_out, gk_out, gv_out,
            q_feat, k_feat, gain, q_slope, k_slope, weighted, grad_att,
-           send_buf, rs_buf, share, fr_send, fr_buf, ag_send, whole,
-           in_sem, out_sem, rs_ssem, rs_rsem, fr_ssem, fr_rsem, ag_ssem, ag_rsem):
+           send_buf, rs_buf, share, zh_send, zh_buf, fr_send, fr_buf, ag_send, whole,
+           in_sem, out_sem, rs_ssem, rs_rsem, zh_ssem, zh_rsem, fr_ssem, fr_rsem, ag_ssem, ag_rsem):
     D = HEAD_DIM
-    owners = 2 * rows_n
+    owners = OWNERS
+    pairs = rows_n // 2
     chips = frames_n // 2
     frame, row = lax.axis_index("frame"), lax.axis_index("row")
     chip, core = frame // 2, frame % 2
-    me = row * 2 + core
+    pair, half = row // 2, row % 2
+    me = half * 2 + core
 
     def column_id(step):
         dest = lax.rem(me + step, owners)
-        return (chip * 2 + dest % 2, dest // 2)
+        return (chip * 2 + dest % 2, pair * 2 + dest // 2)
+
+    def pair_id(step):
+        return (frame, lax.rem(pair + step, pairs) * 2 + half)
 
     def chip_id(step):
         return (lax.rem(chip + step, chips) * 2 + core, row)
@@ -50,6 +57,8 @@
     barrier = pltpu.get_barrier_semaphore()
     for j in range(1, owners):
         pl.semaphore_signal(barrier, inc=1, device_id=column_id(j), device_id_type=MESH)
+    for j in range(1, pairs):
+        pl.semaphore_signal(barrier, inc=1, device_id=pair_id(j), device_id_type=MESH)
     for j in range(1, chips):
         pl.semaphore_signal(barrier, inc=1, device_id=chip_id(j), device_id_type=MESH)
 
@@ -77,6 +86,15 @@
             send_sem=rs_ssem.at[p, g, j], recv_sem=rs_rsem.at[p, g, j],
             device_id=column_id(j), device_id_type=MESH)
 
+    def both(g):
+        return pl.ds(2 * slot_of[g], 2 * pieces[g])
+
+    def zh_copy(p, g, j):
+        return pltpu.make_async_remote_copy(
+            src_ref=zh_send.at[p, both(g)], dst_ref=zh_buf.at[p, j, both(g)],
+            send_sem=zh_ssem.at[p, g, j], recv_sem=zh_rsem.at[p, g, j],
+            device_id=pair_id(j), device_id_type=MESH)
+
     def fr_copy(p, g, j):
         return pltpu.make_async_remote_copy(
             src_ref=fr_send.at[p, slot(g)], dst_ref=fr_buf.at[p, j, slot(g)],
@@ -113,6 +131,20 @@
                 mine = mine + block
             else:
                 other = block if other is None else other + block
+        share[p, 0, slot(g), :] = mine
+        share[p, 1, slot(g), :] = other
+        zh_send[p, both(g), :] = jnp.concatenate([mine, other], axis=0).astype(jnp.bfloat16)
+        for j in range(1, pairs):
+            zh_copy(p, g, j).start()
+
+    def reduce_pairs(p, g):
+        for j in range(1, pairs):
+            zh_copy(p, g, j).wait_recv()
+        mine, other = share[p, 0, slot(g), :], share[p, 1, slot(g), :]
+        for j in range(1, pairs):
+            block = zh_buf[p, j, both(g), :].astype(jnp.float32)
+            mine = mine + block[:pieces[g]]
+            other = other + block[pieces[g]:]
         share[p, 0, slot(g), :] = mine
         share[p, 1, slot(g), :] = other
         fr_send[p, slot(g), :] = (mine + other).astype(jnp.bfloat16)
@@ -154,7 +186,7 @@
             k_slope[h] = slope
             send_buf[0, base_of[g] + i * D:base_of[g] + (i + 1) * D, :D] = dot(feat, val, NT).astype(jnp.bfloat16)
         if g == 0:
-            pl.semaphore_wait(barrier, owners - 1 + chips - 1)
+            pl.semaphore_wait(barrier, owners - 1 + pairs - 1 + chips - 1)
         start_rs(0, g)
 
     loads[2].wait()
@@ -168,12 +200,7 @@
             q_slope[h] = slope
             weighted[h] = g_raw[cols(h), :].astype(jnp.float32) * gain[cols(h), :]
 
-    for g in span:
-        reduce_rows(0, g)
-    for g in span:
-        scan_frames(0, g)
-
-    for g in span:
+    def query_side(g):
         wait_whole(0, g)
         for i, h in enumerate(groups[g]):
             att = dot(head_state(0, g, i), q_feat[h], TN)
@@ -182,29 +209,40 @@
             inner = jnp.mean(w * att, axis=0, keepdims=True)
             ga = (inv * w - att * (inv * inv * inv * inner)).astype(jnp.bfloat16)
             grad_att[h] = ga
-            send_buf[1, base_of[g] + i * D:base_of[g] + (i + 1) * D, :D] = dot(q_feat[h], ga, NT).astype(jnp.bfloat16)
+            row0 = base_of[g] + i * D
+            send_buf[1, row0:row0 + D, :D] = dot(q_feat[h], ga, NT).astype(jnp.bfloat16)
         start_rs(1, g)
 
-    for g in span:
+    def grad_query(g):
         for i, h in enumerate(groups[g]):
             gq = dot(head_state(0, g, i), grad_att[h], NN) * q_slope[h]
             gq_out[cols(h), :] = gq.astype(jnp.bfloat16)
-    stores = [
-        pltpu.make_async_copy(src, dst, out_sem.at[i])
-        for i, (src, dst) in enumerate([(gq_out, gq_hbm), (gk_out, gk_hbm), (gv_out, gv_hbm)])
-    ]
-    stores[0].start()
-
-    for g in span:
-        reduce_rows(1, g)
-    for g in span:
-        scan_frames(1, g)
-    for g in span:
+
+    def key_side(g):
         wait_whole(1, g)
         for i, h in enumerate(groups[g]):
             adj = head_state(1, g, i)
             gv_out[cols(h), :] = dot(adj, k_feat[h], TN).astype(jnp.bfloat16)
             gk_out[cols(h), :] = (dot(adj, v_raw[cols(h), :], NN) * k_slope[h]).astype(jnp.bfloat16)
+
+    def skewed(p, last, beside):
+        stages = [reduce_rows, reduce_pairs, scan_frames]
+        for t in range(len(groups) + len(stages)):
+            for at, stage in enumerate(stages):
+                if 0 <= t - at < len(groups):
+                    stage(p, t - at)
+            if beside is not None and t < len(groups):
+                beside(t)
+            if 0 <= t - len(stages) < len(groups):
+                last(t - len(stages))
+
+    stores = [
+        pltpu.make_async_copy(src, dst, out_sem.at[i])
+        for i, (src, dst) in enumerate([(gq_out, gq_hbm), (gk_out, gk_hbm), (gv_out, gv_hbm)])
+    ]
+    skewed(0, query_side, None)
+    skewed(1, key_side, grad_query)
+    stores[0].start()
     stores[1].start()
     stores[2].start()
 
@@ -213,6 +251,8 @@
             for j in range(1, owners):
                 rs_copy(p, g, j).wait_send()
                 ag_copy(p, g, j).wait_send()
+            for j in range(1, pairs):
+                zh_copy(p, g, j).wait_send()
             for j in range(1, chips):
                 fr_copy(p, g, j).wait_send()
     for c in stores:
@@ -222,9 +262,8 @@
 def body(rows_n, frames_n, query_raw, key_raw, values, norm_gain, grad_out):
     tok, width = query_raw.shape
     heads = width // HEAD_DIM
-    owners, chips = 2 * rows_n, frames_n // 2
-    first = max(1, heads * 4 // 5)
-    groups = [g for g in (list(range(first)), list(range(first, heads))) if g]
+    owners, pairs, chips = OWNERS, rows_n // 2, frames_n // 2
+    groups = [list(range(s, min(s + GROUP, heads))) for s in range(0, heads, GROUP)]
     n = len(groups)
     unit = 16 * owners
     pieces = [-(-len(g) * HEAD_DIM // unit) * 16 for g in groups]
@@ -248,19 +287,22 @@
             pltpu.VMEM((2, owners * piece, LANES), bf),
             pltpu.VMEM((2, owners, piece, LANES), bf),
             pltpu.VMEM((2, 2, piece, LANES), f32),
+            pltpu.VMEM((2, 2 * piece, LANES), bf),
+            pltpu.VMEM((2, pairs, 2 * piece, LANES), bf),
             pltpu.VMEM((2, piece, LANES), bf),
             pltpu.VMEM((2, chips, piece, LANES), bf),
             pltpu.VMEM((2, 2, piece, LANES), bf),
             pltpu.VMEM((2, owners * piece, LANES), bf),
             dma((4,)), dma((3,)),
             dma((2, n, owners)), dma((2, n, owners)),
+            dma((2, n, pairs)), dma((2, n, pairs)),
             dma((2, n, chips)), dma((2, n, chips)),
             dma((2, n, owners)), dma((2, n, owners)),
         ],
         cost_estimate=pl.CostEstimate(
             flops=flops, bytes_accessed=14 * tok * width, transcendentals=2 * tok * width),
         compiler_params=pltpu.CompilerParams(
-            collective_id=0, has_side_effects=True, vmem_limit_bytes=48 * 1024 * 1024),
+            collective_id=0, has_side_effects=True, vmem_limit_bytes=60 * 1024 * 1024),
     )(query_raw.T, key_raw.T, values.T, norm_gain, grad_out.T)
     return tuple(g.T for g in grads)
 

time: 52.9 us -> 50.1 us (0.947)
  local copies, waits for them, and re-layouts: 7.35 us -> 4.04 us
    unnamed x13 -> x7, local copies, waits for them, and re-layouts: 7.35 us -> 4.04 us
    pallas_call x1, Pallas kernels: 44.6 us -> 45.1 us  [body(): pl.pallas_call(functools.partial(kernel, groups, pieces, rows_n, frames_n...]
where the time goes in v3:
time: 50.1 us; the launch traced here: 49.8 us
  Pallas kernels  45.1 us (90%)
  local copies, waits for them, and re-layouts  4.04 us (8%)
  between operations  0.65 us (1%)
    pallas_call x1, Pallas kernels, body(): pl.pallas_call(functools.partial(kernel, groups, pieces, rows_n, frames_n...  45.1 us
    unnamed x7, local copies, waits for them, and re-layouts  4.04 us

profile of v3, /device:TPU:0, one launch (start us, length us, event | category | flops | bytes accessed | tf_op | source)
XLA Modules:
  0.0 49.8 jit_solution(15988522344045198505)
XLA Ops:
  0.6 45.1 %shard_map.76 = (bf16[1120,256]{1,0:T(8,128)(2,1)}, bf16[1120,256]{1,0:T(8,128)(2,1)}, bf16[1120,256]{1,0:T(8,128)(2,1)}) custom-call(bf16[1120,256]{1,0:T(8,128)(2,1)} %bitcast.7, bf16[1120,256]{1,0:T(8,128)(2,1)} %bitcast.8, bf16[1120,256]{1,0:T(8,128)(2,1)} %bitcast.9, f32[1120]{0:T(1024)} %gain_ref.1, bf16[1120,256]{1,0:T(8,128)(2,1)} %bitcast.10), custom_call_target="tpu_custom_call" | custom-call | flops 385351680 | bytes 4014080 | tf_op jit(solution)/shard_map/pallas_call | solution.py:278
  45.8 0.0 copy-start.1
  45.8 2.0 %copy.11 = bf16[256,1120]{0,1:T(8,128)(2,1)} copy(bf16[256,1120]{0,1:T(8,128)(2,1)} %bitcast.13) | data formatting | bytes 1146880
  47.8 0.0 copy-done.1
  47.8 0.0 copy-start
  47.8 0.8 %copy.12 = bf16[256,1120]{0,1:T(8,128)(2,1)} copy(bf16[256,1120]{0,1:T(8,128)(2,1)S(1)} %bitcast.12) | data formatting | bytes 1146880
  48.6 0.5 copy-done
  49.0 0.8 %copy.13 = bf16[256,1120]{0,1:T(8,128)(2,1)} copy(bf16[256,1120]{0,1:T(8,128)(2,1)S(1)} %bitcast.11) | data formatting | bytes 1146880
Async XLA Ops:
  45.8 2.0 %copy-start.1 = (bf16[1120,256]{1,0:T(8,128)(2,1)S(1)}, bf16[1120,256]{1,0:T(8,128)(2,1)}, u32[]{:S(2)}) copy-start(bf16[1120,256]{1,0:T(8,128)(2,1)} %get-tuple-element.7) | copy-start | bytes 1720324
  47.8 1.3 %copy-start = (bf16[1120,256]{1,0:T(8,128)(2,1)S(1)}, bf16[1120,256]{1,0:T(8,128)(2,1)}, u32[]{:S(2)}) copy-start(bf16[1120,256]{1,0:T(8,128)(2,1)} %get-tuple-element.8) | copy-start | bytes 1720324

commit v4 on v3

--- a/solution.py
+++ b/solution.py
@@ -225,23 +225,23 @@
             gv_out[cols(h), :] = dot(adj, k_feat[h], TN).astype(jnp.bfloat16)
             gk_out[cols(h), :] = (dot(adj, v_raw[cols(h), :], NN) * k_slope[h]).astype(jnp.bfloat16)
 
-    def skewed(p, last, beside):
-        stages = [reduce_rows, reduce_pairs, scan_frames]
-        for t in range(len(groups) + len(stages)):
-            for at, stage in enumerate(stages):
-                if 0 <= t - at < len(groups):
-                    stage(p, t - at)
-            if beside is not None and t < len(groups):
-                beside(t)
-            if 0 <= t - len(stages) < len(groups):
-                last(t - len(stages))
+    def staged(p, last, beside):
+        for stage in (reduce_rows, reduce_pairs, scan_frames):
+            for g in span:
+                stage(p, g)
+            if beside is not None and stage is not scan_frames:
+                for g in span:
+                    if (g == 0) == (stage is reduce_rows):
+                        beside(g)
+        for g in span:
+            last(g)
 
     stores = [
         pltpu.make_async_copy(src, dst, out_sem.at[i])
         for i, (src, dst) in enumerate([(gq_out, gq_hbm), (gk_out, gk_hbm), (gv_out, gv_hbm)])
     ]
-    skewed(0, query_side, None)
-    skewed(1, key_side, grad_query)
+    staged(0, query_side, None)
+    staged(1, key_side, grad_query)
     stores[0].start()
     stores[1].start()
     stores[2].start()

time: 50.1 us -> 47.5 us (0.948)
  the two profiles are of different devices: /device:TPU:0 before, /device:TPU:9 now
where the time goes in v4:
time: 47.5 us; the launch traced here: 47.3 us
  Pallas kernels  42.6 us (90%)
  local copies, waits for them, and re-layouts  4.04 us (9%)
  between operations  0.65 us (1%)
    pallas_call x1, Pallas kernels, body(): pl.pallas_call(functools.partial(kernel, groups, pieces, rows_n, frames_n...  42.6 us
    unnamed x7, local copies, waits for them, and re-layouts  4.04 us

profile of v4, /device:TPU:9, one launch (start us, length us, event | category | flops | bytes accessed | tf_op | source)
XLA Modules:
  0.0 47.3 jit_solution(16845436103588299237)
XLA Ops:
  0.6 42.6 %shard_map.76 = (bf16[1120,256]{1,0:T(8,128)(2,1)}, bf16[1120,256]{1,0:T(8,128)(2,1)}, bf16[1120,256]{1,0:T(8,128)(2,1)}) custom-call(bf16[1120,256]{1,0:T(8,128)(2,1)} %bitcast.7, bf16[1120,256]{1,0:T(8,128)(2,1)} %bitcast.8, bf16[1120,256]{1,0:T(8,128)(2,1)} %bitcast.9, f32[1120]{0:T(1024)} %gain_ref.1, bf16[1120,256]{1,0:T(8,128)(2,1)} %bitcast.10), custom_call_target="tpu_custom_call" | custom-call | flops 385351680 | bytes 4014080 | tf_op jit(solution)/shard_map/pallas_call | solution.py:278
  43.2 0.0 copy-start.1
  43.2 2.0 %copy.11 = bf16[256,1120]{0,1:T(8,128)(2,1)} copy(bf16[256,1120]{0,1:T(8,128)(2,1)} %bitcast.13) | data formatting | bytes 1146880
  45.2 0.0 copy-done.1
  45.2 0.0 copy-start
  45.2 0.8 %copy.12 = bf16[256,1120]{0,1:T(8,128)(2,1)} copy(bf16[256,1120]{0,1:T(8,128)(2,1)S(1)} %bitcast.12) | data formatting | bytes 1146880
  46.0 0.5 copy-done
  46.5 0.8 %copy.13 = bf16[256,1120]{0,1:T(8,128)(2,1)} copy(bf16[256,1120]{0,1:T(8,128)(2,1)S(1)} %bitcast.11) | data formatting | bytes 1146880
Async XLA Ops:
  43.2 2.0 %copy-start.1 = (bf16[1120,256]{1,0:T(8,128)(2,1)S(1)}, bf16[1120,256]{1,0:T(8,128)(2,1)}, u32[]{:S(2)}) copy-start(bf16[1120,256]{1,0:T(8,128)(2,1)} %get-tuple-element.7) | copy-start | bytes 1720324
  45.2 1.3 %copy-start = (bf16[1120,256]{1,0:T(8,128)(2,1)S(1)}, bf16[1120,256]{1,0:T(8,128)(2,1)}, u32[]{:S(2)}) copy-start(bf16[1120,256]{1,0:T(8,128)(2,1)} %get-tuple-element.8) | copy-start | bytes 1720324

commit v5 on v4

--- a/solution.py
+++ b/solution.py
@@ -10,7 +10,7 @@
 HEAD_DIM = 112
 LANES = 128
 OWNERS = 4
-GROUP = 4
+GROUP = 5
 MESH = pl.DeviceIdType.MESH
 TN = (((0,), (0,)), ((), ()))
 NT = (((1,), (1,)), ((), ()))

time: 47.5 us -> 48.9 us (1.029)
  Pallas kernels: 42.6 us -> 43.9 us
    pallas_call x1, Pallas kernels: 42.6 us -> 43.9 us  [body(): pl.pallas_call(functools.partial(kernel, groups, pieces, rows_n, frames_n...]
where the time goes in v5:
time: 48.9 us; the launch traced here: 48.6 us
  Pallas kernels  43.9 us (90%)
  local copies, waits for them, and re-layouts  4.04 us (8%)
  between operations  0.65 us (1%)
    pallas_call x1, Pallas kernels, body(): pl.pallas_call(functools.partial(kernel, groups, pieces, rows_n, frames_n...  43.9 us
    unnamed x7, local copies, waits for them, and re-layouts  4.04 us

profile of v5, /device:TPU:9, one launch (start us, length us, event | category | flops | bytes accessed | tf_op | source)
XLA Modules:
  0.0 48.6 jit_solution(12763452788321843405)
XLA Ops:
  0.6 43.9 %shard_map.76 = (bf16[1120,256]{1,0:T(8,128)(2,1)}, bf16[1120,256]{1,0:T(8,128)(2,1)}, bf16[1120,256]{1,0:T(8,128)(2,1)}) custom-call(bf16[1120,256]{1,0:T(8,128)(2,1)} %bitcast.7, bf16[1120,256]{1,0:T(8,128)(2,1)} %bitcast.8, bf16[1120,256]{1,0:T(8,128)(2,1)} %bitcast.9, f32[1120]{0:T(1024)} %gain_ref.1, bf16[1120,256]{1,0:T(8,128)(2,1)} %bitcast.10), custom_call_target="tpu_custom_call" | custom-call | flops 385351680 | bytes 4014080 | tf_op jit(solution)/shard_map/pallas_call | solution.py:278
  44.6 0.0 copy-start.1
  44.6 2.0 %copy.11 = bf16[256,1120]{0,1:T(8,128)(2,1)} copy(bf16[256,1120]{0,1:T(8,128)(2,1)} %bitcast.13) | data formatting | bytes 1146880
  46.5 0.0 copy-done.1
  46.5 0.0 copy-start
  46.5 0.8 %copy.12 = bf16[256,1120]{0,1:T(8,128)(2,1)} copy(bf16[256,1120]{0,1:T(8,128)(2,1)S(1)} %bitcast.12) | data formatting | bytes 1146880
  47.3 0.5 copy-done
  47.8 0.8 %copy.13 = bf16[256,1120]{0,1:T(8,128)(2,1)} copy(bf16[256,1120]{0,1:T(8,128)(2,1)S(1)} %bitcast.11) | data formatting | bytes 1146880
Async XLA Ops:
  44.6 2.0 %copy-start.1 = (bf16[1120,256]{1,0:T(8,128)(2,1)S(1)}, bf16[1120,256]{1,0:T(8,128)(2,1)}, u32[]{:S(2)}) copy-start(bf16[1120,256]{1,0:T(8,128)(2,1)} %get-tuple-element.7) | copy-start | bytes 1720324
  46.5 1.3 %copy-start = (bf16[1120,256]{1,0:T(8,128)(2,1)S(1)}, bf16[1120,256]{1,0:T(8,128)(2,1)}, u32[]{:S(2)}) copy-start(bf16[1120,256]{1,0:T(8,128)(2,1)} %get-tuple-element.8) | copy-start | bytes 1720324

commit v6 on v4

--- a/solution.py
+++ b/solution.py
@@ -200,6 +200,15 @@
             q_slope[h] = slope
             weighted[h] = g_raw[cols(h), :].astype(jnp.float32) * gain[cols(h), :]
 
+    def store(src, dst, g, at):
+        rows = pl.ds(groups[g][0] * D, len(groups[g]) * D)
+        return pltpu.make_async_copy(src.at[rows], dst.at[rows], out_sem.at[at, g])
+
+    stores = [
+        [store(src, dst, g, at) for g in range(len(groups))]
+        for at, (src, dst) in enumerate([(gq_out, gq_hbm), (gk_out, gk_hbm), (gv_out, gv_hbm)])
+    ]
+
     def query_side(g):
         wait_whole(0, g)
         for i, h in enumerate(groups[g]):
@@ -217,6 +226,7 @@
         for i, h in enumerate(groups[g]):
             gq = dot(head_state(0, g, i), grad_att[h], NN) * q_slope[h]
             gq_out[cols(h), :] = gq.astype(jnp.bfloat16)
+        stores[0][g].start()
 
     def key_side(g):
         wait_whole(1, g)
@@ -224,6 +234,8 @@
             adj = head_state(1, g, i)
             gv_out[cols(h), :] = dot(adj, k_feat[h], TN).astype(jnp.bfloat16)
             gk_out[cols(h), :] = (dot(adj, v_raw[cols(h), :], NN) * k_slope[h]).astype(jnp.bfloat16)
+        stores[1][g].start()
+        stores[2][g].start()
 
     def staged(p, last, beside):
         for stage in (reduce_rows, reduce_pairs, scan_frames):
@@ -236,15 +248,8 @@
         for g in span:
             last(g)
 
-    stores = [
-        pltpu.make_async_copy(src, dst, out_sem.at[i])
-        for i, (src, dst) in enumerate([(gq_out, gq_hbm), (gk_out, gk_hbm), (gv_out, gv_hbm)])
-    ]
     staged(0, query_side, None)
     staged(1, key_side, grad_query)
-    stores[0].start()
-    stores[1].start()
-    stores[2].start()
 
     for p in range(2):
         for g in span:
@@ -255,7 +260,7 @@
                 zh_copy(p, g, j).wait_send()
             for j in range(1, chips):
                 fr_copy(p, g, j).wait_send()
-    for c in stores:
+    for c in sum(stores, []):
         c.wait()
 
 
@@ -293,7 +298,7 @@
             pltpu.VMEM((2, chips, piece, LANES), bf),
             pltpu.VMEM((2, 2, piece, LANES), bf),
             pltpu.VMEM((2, owners * piece, LANES), bf),
-            dma((4,)), dma((3,)),
+            dma((4,)), dma((3, n)),
             dma((2, n, owners)), dma((2, n, owners)),
             dma((2, n, pairs)), dma((2, n, pairs)),
             dma((2, n, chips)), dma((2, n, chips)),

time: 47.5 us -> 47.3 us (level)
  the two profiles are of different devices: /device:TPU:9 before, /device:TPU:0 now
where the time goes in v6:
time: 47.3 us; the launch traced here: 46.6 us
  Pallas kernels  41.9 us (89%)
  local copies, waits for them, and re-layouts  4.04 us (9%)
  between operations  0.65 us (1%)
    pallas_call x1, Pallas kernels, body(): pl.pallas_call(functools.partial(kernel, groups, pieces, rows_n, frames_n...  41.9 us
    unnamed x7, local copies, waits for them, and re-layouts  4.04 us

profile of v6, /device:TPU:0, one launch (start us, length us, event | category | flops | bytes accessed | tf_op | source)
XLA Modules:
  0.0 46.6 jit_solution(16591181754612549254)
XLA Ops:
  0.6 41.9 %shard_map.76 = (bf16[1120,256]{1,0:T(8,128)(2,1)}, bf16[1120,256]{1,0:T(8,128)(2,1)}, bf16[1120,256]{1,0:T(8,128)(2,1)}) custom-call(bf16[1120,256]{1,0:T(8,128)(2,1)} %bitcast.7, bf16[1120,256]{1,0:T(8,128)(2,1)} %bitcast.8, bf16[1120,256]{1,0:T(8,128)(2,1)} %bitcast.9, f32[1120]{0:T(1024)} %gain_ref.1, bf16[1120,256]{1,0:T(8,128)(2,1)} %bitcast.10), custom_call_target="tpu_custom_call" | custom-call | flops 385351680 | bytes 4014080 | tf_op jit(solution)/shard_map/pallas_call | solution.py:283
  42.6 0.0 copy-start.1
  42.6 2.0 %copy.11 = bf16[256,1120]{0,1:T(8,128)(2,1)} copy(bf16[256,1120]{0,1:T(8,128)(2,1)} %bitcast.13) | data formatting | bytes 1146880
  44.6 0.0 copy-done.1
  44.6 0.0 copy-start
  44.6 0.8 %copy.12 = bf16[256,1120]{0,1:T(8,128)(2,1)} copy(bf16[256,1120]{0,1:T(8,128)(2,1)S(1)} %bitcast.12) | data formatting | bytes 1146880
  45.4 0.5 copy-done
  45.8 0.8 %copy.13 = bf16[256,1120]{0,1:T(8,128)(2,1)} copy(bf16[256,1120]{0,1:T(8,128)(2,1)S(1)} %bitcast.11) | data formatting | bytes 1146880
Async XLA Ops:
  42.6 2.0 %copy-start.1 = (bf16[1120,256]{1,0:T(8,128)(2,1)S(1)}, bf16[1120,256]{1,0:T(8,128)(2,1)}, u32[]{:S(2)}) copy-start(bf16[1120,256]{1,0:T(8,128)(2,1)} %get-tuple-element.7) | copy-start | bytes 1720324
  44.6 1.3 %copy-start = (bf16[1120,256]{1,0:T(8,128)(2,1)S(1)}, bf16[1120,256]{1,0:T(8,128)(2,1)}, u32[]{:S(2)}) copy-start(bf16[1120,256]{1,0:T(8,128)(2,1)} %get-tuple-element.8) | copy-start | bytes 1720324
